TPU v7x, 512 devices: a whole 4x4x16 slice. The times are simulated.
512 devices in a mesh: pts: 64 (over z, x), cand: 8 (over y, core).
Axes of the slice: x: 4, y: 4, z: 16, core: 2. Of those that a mesh axis runs over, the one named last changes fastest.
Arguments:
- points: float32 [131072, 512], P('pts'), may hold values from -10 to 10
- prior_min: float32 [131072], P('pts'), may hold values from 0.05 to 6
- cand_slots: int32 [64, 8, 32], P('pts', 'cand'), may hold values from -1 to 2047, as said below
Outputs:
- new_min: float32 [131072], P('pts')
- cost: float32 [], replicated
Inputs may be any that keep to these rules, and one draw needn't show every extreme that they name: `cand_slots`: in each [o, b] row the live entries come first, 1 to 32 of them, and are distinct local rows, distinct over all b of one owner; some [o, b] row is full.
All inputs are finite; a program needn't handle non-finite values.
Results may differ from a plain program's by a relative error of at most 0.0003.
Values sent between devices are 32-bit elements; how exact they have to be, the bound alone decides.
A program may use at most 64 MiB of HBM per device.

v0:
```python
import jax
import jax.numpy as jnp
from jax import lax
from jax.sharding import PartitionSpec as P


def distances(points, pnorm, rows, cnorm):
    dots = jnp.dot(
        points, rows.T, precision=lax.Precision.HIGHEST, preferred_element_type=jnp.float32
    )
    dist = (pnorm[:, None] + cnorm[None, :] - 2.0 * dots) / points.shape[1]
    return jnp.min(dist, axis=1)


def local(points, prior_min, cand_slots):
    count = points.shape[0]
    slots = cand_slots.reshape(-1)
    live = slots >= 0
    picked = jnp.take(points, jnp.maximum(slots, 0), axis=0) * live[:, None].astype(jnp.float32)
    norms = jnp.where(live, jnp.sum(picked * picked, axis=1), jnp.float32(1e30))
    pnorm = jnp.sum(points * points, axis=1)
    rows, cnorm = (
        lax.all_gather(picked, "pts", axis=0, tiled=True),
        lax.all_gather(norms, "pts", axis=0, tiled=True),
    )
    local_min = distances(points, pnorm, rows, cnorm)
    total_points = count * lax.axis_size("pts")
    found = lax.pmin(local_min, "cand")
    new_min = jnp.minimum(prior_min, found)
    cost = lax.psum(jnp.sum(new_min), "pts") / total_points
    return (new_min, cost)


def solution(mesh):
    placed = (P("pts", None), P("pts"), P("pts", "cand", None))
    return jax.shard_map(
        local, mesh=mesh, in_specs=placed, out_specs=(P("pts"), P()), check_vma=False
    )
```

profile of v0, /device:TPU:2, one launch (start us, length us, event | category | flops | bytes accessed | tf_op | source)
XLA Modules:
  0.0 362.3 jit_solution(15876892631275661497)
XLA Ops:
  7.2 0.0 all-gather.2.cloned.1.call-start
  7.2 0.7 compare_bitcast_fusion
  7.9 0.7 maximum_bitcast_fusion
  8.5 2.8 gather_fusion
  11.4 0.8 multiply_reduce_fusion.1
  12.2 0.0 all-gather.2.cloned.1.call-update
  12.2 1.3 dynamic-slice
  14.1 0.8 fusion.2
  14.9 148.3 %all-reduce = f32[2048]{0:T(1024)S(1)} all-reduce(f32[2048]{0:T(1024)S(1)} %fusion.2), channel_id=1, replica_groups=mesh['pts'=64,'cand'=8] {'pts'}, use_global_device_ids=true, to_apply=%add | all-reduce | flops 2048 | bytes 16384
  163.2 2.5 multiply_reduce_fusion
  165.7 0.0 copy-start
  165.7 0.0 all-gather.2.cloned.1.call-done
  165.8 30.8 %fusion.1 = f32[2048]{0:T(1024)S(1)} fusion(f32[2048,512]{1,0:T(8,128)} %all-gather.2.cloned.1.call-done, f32[2048,512]{1,0:T(8,128)} %param.3, f32[2048]{0:T(1024)S(1)} %all-reduce, f32[2048]{0:T(1024)S(1)} %multiply_reduce_fusion), kind=kOutput, calls=%fused_computation.3 | convolution fusion | flops 25790773248 | bytes 8413184 | tf_op jit(solution)/shard_map/dot_general | solution.py:8
  196.6 12.7 %pmin.7 = f32[2048]{0:T(1024)S(1)} all-reduce(f32[2048]{0:T(1024)S(1)} %fusion.1), channel_id=1, replica_groups=mesh['pts'=64,'cand'=8] {'cand'}, use_global_device_ids=true, to_apply=%region_3.4 | all-reduce | flops 2048 | bytes 16384 | tf_op jit(solution)/shard_map/pmin | solution.py:28
  209.3 0.0 copy-done
  209.3 1.2 fusion.3
  210.5 143.1 %psum.7 = f32[]{:T(128)} all-reduce(f32[]{:T(128)} %get-tuple-element.2), channel_id=1, replica_groups=mesh['pts'=64,'cand'=8] {'pts'}, use_global_device_ids=true, to_apply=%region_5.6 | all-reduce | flops 1 | bytes 8 | tf_op jit(solution)/shard_map/psum | solution.py:30
  (2 shorter events, 0.0 us)
Async XLA Ops:
  7.2 158.6 %all-gather.2.cloned.1.call-start = ((), (), s32[]{:S(2)}) async-start(), calls=%async_computation | async-start | bytes 4259840 | tf_op jit(solution)/shard_map/all_gather | solution.py:23
  165.7 43.6 %copy-start = (f32[2048]{0:T(1024)S(1)}, f32[2048]{0:T(1024)}, u32[]{:S(2)}) copy-start(f32[2048]{0:T(1024)} %param.4) | copy-start | bytes 24580
Sparse Core Ops, SparseCore 0:
  12.3 149.4 all-gather.1
where the time goes:
time: 363 us; the launch traced here: 362 us
  blocking collectives  304 us (84%)
  matrix products  30.8 us (8%)
  between operations  16.5 us (5%)
  other arithmetic  6.66 us (2%)
  local copies, waits for them, and re-layouts  4.09 us (1%)
    unnamed x1, blocking collectives  148 us
    psum x1, blocking collectives, local(): cost = lax.psum(jnp.sum(new_min), 'pts') / total_points  143 us
    dot_general x1, matrix products, distances(): jnp.dot(points, rows.T, precision=lax.Precision.HIGHEST, preferred_elemen...  30.8 us
    pmin x1, blocking collectives, local(): found = lax.pmin(local_min, 'cand')  12.7 us
  transfers between devices with their start and end apart: 1, of which 0 were waited for; matrix products, arithmetic and copies ran while one was open for 1% of the time, Pallas kernels for 0%

commit v1 on v0

v1 whole, which is shorter than its diff:
```python
import functools

import jax
import jax.numpy as jnp
from jax import lax
from jax.experimental import pallas as pl
from jax.experimental.pallas import tpu as pltpu
from jax.sharding import PartitionSpec as P

MESH = pl.DeviceIdType.MESH
NX, NZ, NC = 4, 16, 8
HALF = NZ // 2
RA, RB = 8, 24
F32, BF16 = jnp.float32, jnp.bfloat16


def kernel(
    pts_hbm, prior_ref, slots_ref, out_ref, cost_ref,
    pf, p3, pn, ga, gb, c3, cnb, acc, mins, sx, sz,
    load_sem, ssem, rbz, raz, rx, rr, rax, rbx, s0, scm, rcm, scx, rcx, scz, rcz,
):
    p, c = lax.axis_index("pts"), lax.axis_index("cand")
    z, x = p // NX, p % NX
    npts, width = pf.shape
    quarter = npts // 4

    def peer(dz, dx):
        return (lax.rem(z + dz + NZ, NZ) * NX + lax.rem(x + dx + NX, NX), c)

    def mate(j):
        return (p, lax.rem(c + j, NC))

    def remote(src, dst, send, recv, where):
        return pltpu.make_async_remote_copy(
            src_ref=src, dst_ref=dst, send_sem=send, recv_sem=recv,
            device_id=where, device_id_type=MESH,
        )

    loads = []
    for q in range(4):
        rows = pl.ds(q * quarter, quarter)
        load = pltpu.make_async_copy(pts_hbm.at[rows], pf.at[rows], load_sem.at[q])
        load.start()
        loads.append(load)

    barrier = pltpu.get_barrier_semaphore()
    near = [peer(1, 0), peer(-1, 0), peer(0, 1), peer(0, -1), peer(0, 2)]
    near += [mate(j) for j in range(1, NC)]
    for who in near:
        pl.semaphore_signal(barrier, inc=1, device_id=who, device_id_type=MESH)
    acc[...] = jnp.full(acc.shape, 3e38, F32)
    for load in loads:
        load.wait()
    pl.semaphore_wait(barrier, len(near))

    first = slots_ref[0]
    for i in range(RA + RB):
        slot = slots_ref[i]
        row = pf[pl.ds(jnp.where(slot >= 0, slot, first), 1), :]
        if i < RA:
            ga[0, 0, i : i + 1, :] = row
        else:
            gb[0, 0, i - RA : i - RA + 1, :] = row

    def up(t):
        return jnp.maximum(2 * t - 1, 0)

    def bz_up(t):
        return remote(gb.at[0, up(t)], gb.at[0, 2 * t + 1], ssem.at[0], rbz.at[0, t + 1], peer(-1, 0))

    def bz_dn(t):
        return remote(gb.at[0, 2 * t], gb.at[0, 2 * t + 2], ssem.at[1], rbz.at[1, t + 1], peer(1, 0))

    def az_up(t):
        return remote(ga.at[up(t)], ga.at[2 * t + 1], ssem.at[2], raz.at[0, t + 1], peer(-1, 0))

    def az_dn(t):
        return remote(ga.at[2 * t], ga.at[2 * t + 2], ssem.at[3], raz.at[1, t + 1], peer(1, 0))

    def xr(t):
        two = pl.ds(2 * t - 1, 2)
        return remote(gb.at[0, two], gb.at[3, two], ssem.at[4], rx.at[0, t], peer(0, 1))

    def xl(t):
        two = pl.ds(2 * t - 1, 2)
        return remote(gb.at[0, two], gb.at[1, two], ssem.at[5], rx.at[1, t], peer(0, -1))

    def rel_r(t):
        return remote(gb.at[3, 2 * t - 1], gb.at[2, 2 * t - 1], ssem.at[6], rr.at[0, t], peer(0, 1))

    def rel_l(t):
        return remote(gb.at[1, 2 * t], gb.at[2, 2 * t], ssem.at[7], rr.at[1, t], peer(0, -1))

    own_a = [
        remote(ga.at[0, 0], ga.at[0, d], s0.at[i], rax.at[i], peer(0, -d))
        for i, d in enumerate((3, 1, 2))
    ]
    own_b = [
        remote(gb.at[0, 0], gb.at[d, 0], s0.at[3 + i], rbx.at[i], peer(0, -d))
        for i, d in enumerate((3, 1, 2))
    ]
    last_b = [
        remote(gb.at[0, 15], gb.at[d, 15], s0.at[6 + i], rbx.at[3 + i], peer(0, -d))
        for i, d in enumerate((3, 1, 2))
    ]

    bz_up(0).start()
    bz_dn(0).start()
    for copy in own_a:
        copy.start()
    for copy in own_b:
        copy.start()

    for q in range(npts // 256):
        cols = pl.ds(q * 256, 256)
        t = pf[cols, :].T
        pn[:, cols] = jnp.sum(t * t, axis=0, keepdims=True)
        t = t * -2.0
        hi = t.astype(BF16)
        lo = (t - hi.astype(F32)).astype(BF16)
        p3[0:width, cols] = hi
        p3[width : 2 * width, cols] = lo
        p3[2 * width : 3 * width, cols] = hi

    for copy in own_a:
        copy.wait_recv()
    az_up(0).start()
    az_dn(0).start()
    for copy in own_b:
        copy.wait_recv()

    def fill(at, pieces):
        rows = pieces[0] if len(pieces) == 1 else jnp.concatenate(pieces, axis=0)
        n = rows.shape[0]
        sq = rows * rows
        sq = sum(sq[:, 128 * i : 128 * i + 128] for i in range(width // 128))
        cnb[at : at + n, :] = jnp.broadcast_to(jnp.sum(sq, axis=1, keepdims=True), (n, 128))
        hi = rows.astype(BF16)
        c3[at : at + n, 0:width] = hi
        c3[at : at + n, width : 2 * width] = hi
        c3[at : at + n, 2 * width : 3 * width] = (rows - hi.astype(F32)).astype(BF16)

    def nearest(n):
        d = jnp.dot(c3[0:n, :], p3[...], preferred_element_type=F32)
        d = d + jnp.concatenate([cnb[0:n, :]] * (npts // 128), axis=1)
        acc[...] = jnp.minimum(acc[...], jnp.min(d.reshape(n // 8, 8, npts), axis=0))

    fill(112, [gb[0, 0], gb[1, 0], gb[2, 0], gb[3, 0]])
    fill(208, [ga[0].reshape(NX * RA, width), ga[0, 0], ga[0, 0]])

    def tick(t, _):
        bz_up(t - 1).wait_recv()

        @pl.when(t < HALF)
        def _():
            bz_dn(t - 1).wait_recv()

        bz_up(t - 1).wait_send()

        @pl.when(t < HALF)
        def _():
            bz_dn(t - 1).wait_send()

        @pl.when(t < HALF)
        def _():
            bz_up(t).start()

        @pl.when(t < HALF - 1)
        def _():
            bz_dn(t).start()

        @pl.when(t > 1)
        def _():
            xr(t - 1).wait_send()
            xl(t - 1).wait_send()

        @pl.when(t < HALF)
        def _():
            xr(t).start()
            xl(t).start()

        @pl.when(t == HALF)
        def _():
            for copy in last_b:
                copy.start()

        az_dn(t - 1).wait_recv()

        @pl.when(t < HALF)
        def _():
            az_up(t - 1).wait_recv()

        @pl.when(t < HALF)
        def _():
            az_up(t - 1).wait_send()

        az_dn(t - 1).wait_send()

        @pl.when(t < HALF)
        def _():
            az_dn(t).start()

        @pl.when(t < HALF - 1)
        def _():
            az_up(t).start()

        @pl.when(t >= 2)
        def _():
            xr(t - 1).wait_recv()
            xl(t - 1).wait_recv()

        @pl.when(t >= 3)
        def _():
            rel_r(t - 2).wait_send()
            rel_l(t - 2).wait_send()

        @pl.when(t >= 2)
        def _():
            rel_r(t - 1).start()
            rel_l(t - 1).start()

        @pl.when(t >= 3)
        def _():
            rel_r(t - 2).wait_recv()
            rel_l(t - 2).wait_recv()

        @pl.when(t < HALF)
        def _():
            fill(0, [ga[2 * t - 1].reshape(NX * RA, width), ga[2 * t].reshape(NX * RA, width)])
            fill(64, [gb[0, 2 * t - 1], gb[0, 2 * t]])

        @pl.when(t == HALF)
        def _():
            fill(32, [ga[2 * HALF].reshape(NX * RA, width)])
            fill(64, [gb[0, 15], gb[0, 15]])

        @pl.when(t >= 2)
        def _():
            fill(112, [gb[3, 2 * t - 3], gb[3, 2 * t - 2], gb[1, 2 * t - 3], gb[1, 2 * t - 2]])

        @pl.when(t >= 3)
        def _():
            fill(208, [gb[2, 2 * t - 5], gb[2, 2 * t - 4]])

        nearest(256)
        return 0

    lax.fori_loop(1, HALF + 1, tick, 0)

    for copy in own_a + own_b:
        copy.wait_send()
    rel_r(HALF - 1).wait_send()
    rel_l(HALF - 1).wait_send()
    rel_r(HALF - 1).wait_recv()
    rel_l(HALF - 1).wait_recv()
    for copy in last_b:
        copy.wait_recv()
    fill(0, [gb[2, 13], gb[2, 14], gb[1, 15], gb[3, 15], gb[2, 15], gb[2, 15, 0:8]])
    nearest(128)

    low = jnp.min(acc[...], axis=0, keepdims=True)
    low = (low + pn[...]) / width
    for i in range(npts // 128):
        mins[0, i : i + 1, :] = low[:, 128 * i : 128 * i + 128]
    swaps = [remote(mins.at[0], mins.at[j], scm.at[j], rcm.at[j], mate(j)) for j in range(1, NC)]
    for copy in swaps:
        copy.start()
    for copy in last_b:
        copy.wait_send()
    new = jnp.minimum(prior_ref[...], mins[0])
    for copy in swaps:
        copy.wait_recv()
    for j in range(1, NC):
        new = jnp.minimum(new, mins[j])
    out_ref[...] = new

    sx[x] = jnp.sum(new, axis=0, keepdims=True)
    sums = [
        remote(sx.at[x], sx.at[x], scx.at[d], rcx.at[d], peer(0, d)) for d in range(1, NX)
    ]
    for copy in sums:
        copy.start()
    for copy in swaps:
        copy.wait_send()
    for d in range(1, NX):
        src = lax.rem(x - d + NX, NX)
        remote(sx.at[x], sx.at[src], scx.at[d], rcx.at[d], peer(0, d)).wait_recv()
    sz[z] = (sx[0] + sx[1]) + (sx[2] + sx[3])
    sumz = [
        remote(sz.at[z], sz.at[z], scz.at[d], rcz.at[d], peer(d, 0)) for d in range(1, NZ)
    ]
    for copy in sumz:
        copy.start()
    for copy in sums:
        copy.wait_send()
    for d in range(1, NZ):
        src = lax.rem(z - d + NZ, NZ)
        remote(sz.at[z], sz.at[src], scz.at[d], rcz.at[d], peer(d, 0)).wait_recv()
    total = sz[0]
    for i in range(1, NZ):
        total = total + sz[i]
    cost_ref[...] = jnp.broadcast_to(
        jnp.sum(total, axis=1, keepdims=True) / (npts * NZ * NX), cost_ref.shape
    )
    for copy in sumz:
        copy.wait_send()


def local(points, prior_min, cand_slots):
    npts, width = points.shape
    vmem = pl.BlockSpec(memory_space=pltpu.VMEM)
    dma = pltpu.SemaphoreType.DMA
    new, cost = pl.pallas_call(
        kernel,
        out_shape=(
            jax.ShapeDtypeStruct((npts // 128, 128), F32),
            jax.ShapeDtypeStruct((1, 128), F32),
        ),
        in_specs=[
            pl.BlockSpec(memory_space=pl.ANY), vmem, pl.BlockSpec(memory_space=pltpu.SMEM),
        ],
        out_specs=(vmem, vmem),
        scratch_shapes=[
            pltpu.VMEM((npts, width), F32),
            pltpu.VMEM((3 * width, npts), BF16),
            pltpu.VMEM((1, npts), F32),
            pltpu.VMEM((NZ + 1, NX, RA, width), F32),
            pltpu.VMEM((NX, NZ, RB, width), F32),
            pltpu.VMEM((256, 3 * width), BF16),
            pltpu.VMEM((256, 128), F32),
            pltpu.VMEM((8, npts), F32),
            pltpu.VMEM((NC, npts // 128, 128), F32),
            pltpu.VMEM((NX, 1, 128), F32),
            pltpu.VMEM((NZ, 1, 128), F32),
            dma((4,)), dma((8,)),
            dma((2, HALF + 1)), dma((2, HALF + 1)), dma((2, HALF + 1)), dma((2, HALF + 1)),
            dma((3,)), dma((6,)), dma((9,)),
            dma((NC,)), dma((NC,)), dma((NX,)), dma((NX,)), dma((NZ,)), dma((NZ,)),
        ],
        compiler_params=pltpu.CompilerParams(
            collective_id=0, has_side_effects=True, vmem_limit_bytes=48 << 20
        ),
    )(points, prior_min.reshape(npts // 128, 128), cand_slots.reshape(-1))
    return new.reshape(-1), cost[0, 0]


def solution(mesh):
    placed = (P("pts", None), P("pts"), P("pts", "cand", None))
    return jax.shard_map(
        local, mesh=mesh, in_specs=placed, out_specs=(P("pts"), P()), check_vma=False
    )
```

time: 363 us -> 75.7 us (0.21)
  the two profiles are of different devices: /device:TPU:2 before, /device:TPU:1 now
where the time goes in v1:
time: 75.7 us; the launch traced here: 75.5 us
  Pallas kernels  69.5 us (92%)
  local copies, waits for them, and re-layouts  4.13 us (5%)
  between operations  1.81 us (2%)
    pallas_call x1, Pallas kernels, local(): pl.pallas_call(kernel, out_shape=(jax.ShapeDtypeStruct((npts // 128, 128)...  69.5 us
    unnamed x7, local copies, waits for them, and re-layouts  4.13 us

profile of v1, /device:TPU:1, one launch (start us, length us, event | category | flops | bytes accessed | tf_op | source)
XLA Modules:
  0.0 75.5 jit_solution(5820555156695546141)
XLA Ops:
  0.6 0.0 copy-start
  0.6 2.2 %copy-done = f32[2048,512]{1,0:T(8,128)S(1)} copy-done((f32[2048,512]{1,0:T(8,128)S(1)}, f32[2048,512]{1,0:T(8,128)}, u32[]{:S(2)}) %copy-start) | copy-done | bytes 4194328
  2.8 0.0 copy-start.1
  2.8 0.7 copy-done.1
  3.5 0.0 copy-start.2
  3.5 0.7 copy-done.2
  4.2 69.5 %shard_map.50 = (f32[16,128]{1,0:T(8,128)S(1)}, f32[1,128]{1,0:T(1,128)S(1)}) custom-call(f32[2048,512]{1,0:T(8,128)S(1)} %copy-done, f32[16,128]{1,0:T(8,128)S(1)} %bitcast.5, s32[32]{0:T(128)S(1)} %bitcast.7), custom_call_target="tpu_custom_call" | custom-call | tf_op jit(solution)/shard_map/pallas_call | solution.py:313
  73.7 0.6 copy.7
Async XLA Ops:
  0.6 2.2 %copy-start = (f32[2048,512]{1,0:T(8,128)S(1)}, f32[2048,512]{1,0:T(8,128)}, u32[]{:S(2)}) copy-start(f32[2048,512]{1,0:T(8,128)} %pts_hbm.1) | copy-start | bytes 12582916
  2.8 0.7 copy-start.1
  3.5 0.7 copy-start.2

commit v2 on v1

v2 whole, which is shorter than its diff:
```python
import functools

import jax
import jax.numpy as jnp
from jax import lax
from jax.experimental import pallas as pl
from jax.experimental.pallas import tpu as pltpu
from jax.sharding import PartitionSpec as P

MESH = pl.DeviceIdType.MESH
NX, NZ, NC = 4, 16, 8
HALF = NZ // 2
RA, RB = 8, 24
SPLIT = 2
F32, BF16 = jnp.float32, jnp.bfloat16


def kernel(
    pts_hbm, prior_hbm, slots_hbm, out_ref, cost_ref,
    slots_ref, prior_ref, pf, p3, pn, own, ga, gb, c3, cnb, acc, mins, sx, sz,
    load_sem, ssem, rown, rall, rx, rr, rax, rbx, s0, scm, rcm, scx, rcx, scz, rcz,
):
    p, c = lax.axis_index("pts"), lax.axis_index("cand")
    z, x = p // NX, p % NX
    npts, width = pf.shape
    quarter = npts // 4

    def peer(dz, dx):
        return (lax.rem(z + dz + NZ, NZ) * NX + lax.rem(x + dx + NX, NX), c)

    def mate(j):
        return (p, lax.rem(c + j, NC))

    def remote(src, dst, send, recv, where):
        return pltpu.make_async_remote_copy(
            src_ref=src, dst_ref=dst, send_sem=send, recv_sem=recv,
            device_id=where, device_id_type=MESH,
        )

    loads = []
    for q in range(4):
        rows = pl.ds(q * quarter, quarter)
        load = pltpu.make_async_copy(pts_hbm.at[rows], pf.at[rows], load_sem.at[q])
        load.start()
        loads.append(load)

    barrier = pltpu.get_barrier_semaphore()
    near = [peer(1, 0), peer(-1, 0), peer(0, 1), peer(0, -1), peer(0, 2)]
    near += [mate(j) for j in range(1, NC)]
    for who in near:
        pl.semaphore_signal(barrier, inc=1, device_id=who, device_id_type=MESH)
    slots_copy = pltpu.make_async_copy(slots_hbm, slots_ref, load_sem.at[4])
    slots_copy.start()
    prior_copy = pltpu.make_async_copy(prior_hbm, prior_ref, load_sem.at[5])
    prior_copy.start()
    acc[...] = jnp.full(acc.shape, 3e38, F32)
    slots_copy.wait()
    prior_copy.wait()
    for load in loads:
        load.wait()

    first = slots_ref[0]
    for i in range(RA + RB):
        slot = slots_ref[i]
        own[0, i : i + 1, :] = pf[pl.ds(jnp.where(slot >= 0, slot, first), 1), :]

    pl.semaphore_wait(barrier, len(near))

    def up(t):
        return jnp.maximum(2 * t - 1, 0)

    def sent(kind, t):
        return ssem.at[kind, lax.rem(t, 2)]

    parts = [pl.ds(i * (RA + RB) // SPLIT, (RA + RB) // SPLIT) for i in range(SPLIT)]

    def own_up(i, t):
        src, dst = own.at[up(t), parts[i]], own.at[2 * t + 1, parts[i]]
        return remote(src, dst, sent(i, t), rown.at[i, 0, t + 1], peer(-1, 0))

    def own_dn(i, t):
        src, dst = own.at[2 * t, parts[i]], own.at[2 * t + 2, parts[i]]
        return remote(src, dst, sent(2 + i, t), rown.at[i, 1, t + 1], peer(1, 0))

    def all_up(t):
        return remote(ga.at[up(t)], ga.at[2 * t + 1], sent(4, t), rall.at[0, t + 1], peer(-1, 0))

    def all_dn(t):
        return remote(ga.at[2 * t], ga.at[2 * t + 2], sent(5, t), rall.at[1, t + 1], peer(1, 0))

    def xr(t):
        two = pl.ds(2 * t - 1, 2)
        src = own.at[two, pl.ds(RA, RB)]
        return remote(src, gb.at[2, two], sent(6, t), rx.at[0, t], peer(0, 1))

    def xl(t):
        two = pl.ds(2 * t - 1, 2)
        src = own.at[two, pl.ds(RA, RB)]
        return remote(src, gb.at[0, two], sent(7, t), rx.at[1, t], peer(0, -1))

    def rel_r(t):
        at = 2 * t - 1
        return remote(gb.at[2, at], gb.at[1, at], sent(8, t), rr.at[0, t], peer(0, 1))

    def rel_l(t):
        return remote(gb.at[0, 2 * t], gb.at[1, 2 * t], sent(9, t), rr.at[1, t], peer(0, -1))

    around = (3, 1, 2)
    own_a = [
        remote(own.at[0, pl.ds(0, RA)], ga.at[0, d - 1], s0.at[i], rax.at[i], peer(0, -d))
        for i, d in enumerate(around)
    ]
    own_b = [
        remote(own.at[0, pl.ds(RA, RB)], gb.at[d - 1, 0], s0.at[3 + i], rbx.at[i], peer(0, -d))
        for i, d in enumerate(around)
    ]
    far = 2 * HALF - 1
    last_b = [
        remote(own.at[far, pl.ds(RA, RB)], gb.at[d - 1, far], s0.at[6 + i], rbx.at[3 + i], peer(0, -d))
        for i, d in enumerate(around)
    ]

    for copy in own_a:
        copy.start()
    for i in range(SPLIT):
        own_up(i, 0).start()
        own_dn(i, 0).start()
    for copy in own_b:
        copy.start()

    for q in range(npts // 256):
        cols = pl.ds(q * 256, 256)
        t = pf[cols, :].T
        pn[:, cols] = jnp.sum(t * t, axis=0, keepdims=True)
        t = t * -2.0
        hi = t.astype(BF16)
        lo = (t - hi.astype(F32)).astype(BF16)
        p3[0:width, cols] = hi
        p3[width : 2 * width, cols] = lo
        p3[2 * width : 3 * width, cols] = hi

    def fill(at, pieces):
        rows = pieces[0] if len(pieces) == 1 else jnp.concatenate(pieces, axis=0)
        n = rows.shape[0]
        sq = rows * rows
        sq = sum(sq[:, 128 * i : 128 * i + 128] for i in range(width // 128))
        cnb[at : at + n, :] = jnp.broadcast_to(jnp.sum(sq, axis=1, keepdims=True), (n, 128))
        hi = rows.astype(BF16)
        c3[at : at + n, 0:width] = hi
        c3[at : at + n, width : 2 * width] = hi
        c3[at : at + n, 2 * width : 3 * width] = (rows - hi.astype(F32)).astype(BF16)

    def nearest(at, n):
        d = jnp.dot(c3[at : at + n, :], p3[...], preferred_element_type=F32)
        d = d + jnp.concatenate([cnb[at : at + n, :]] * (npts // 128), axis=1)
        acc[...] = jnp.minimum(acc[...], jnp.min(d.reshape(n // 8, 8, npts), axis=0))

    def others(pos):
        return ga[pos].reshape((NX - 1) * RA, width)

    fill(208, [own[0], own[0, 0:16]])
    for copy in own_a:
        copy.wait_recv()
    all_dn(0).start()
    all_up(0).start()

    def tick(t, _):
        for i in range(SPLIT):
            own_up(i, t - 1).wait_recv()

            @pl.when(t < HALF)
            def _():
                own_up(i, t).start()
                own_dn(i, t - 1).wait_recv()

            @pl.when(t < HALF - 1)
            def _():
                own_dn(i, t).start()

        @pl.when(t < HALF)
        def _():
            xr(t).start()
            xl(t).start()
            fill(0, [own[2 * t - 1], own[2 * t]])

        @pl.when(t == HALF)
        def _():
            for copy in last_b:
                copy.start()
            fill(0, [own[far], own[far]])

        @pl.when(t == 1)
        def _():
            for copy in own_b:
                copy.wait_recv()
            fill(64, [gb[0, 0], gb[1, 0], gb[2, 0], others(0)])

        @pl.when(t >= 3)
        def _():
            fill(64, [gb[2, 2 * t - 5], gb[2, 2 * t - 4], gb[0, 2 * t - 5], gb[0, 2 * t - 4]])

        nearest(0, 160)

        @pl.when(t == HALF)
        def _():
            relay(t - 1)

        all_dn(t - 1).wait_recv()

        @pl.when(t < HALF)
        def _():
            all_dn(t).start()
            all_up(t - 1).wait_recv()

        @pl.when(t < HALF - 1)
        def _():
            all_up(t).start()

        @pl.when(t < HALF)
        def _():
            fill(160, [others(2 * t - 1), others(2 * t)])

        @pl.when(t == HALF)
        def _():
            fill(160, [others(2 * HALF), others(2 * HALF)])

        @pl.when(t >= 4)
        def _():
            rel_r(t - 3).wait_recv()
            rel_l(t - 3).wait_recv()
            fill(208, [gb[1, 2 * t - 7], gb[1, 2 * t - 6]])

        nearest(160, 96)

        @pl.when((t >= 2) & (t < HALF))
        def _():
            relay(t - 1)

        for i in range(SPLIT):
            own_up(i, t - 1).wait_send()
        all_dn(t - 1).wait_send()

        @pl.when(t < HALF)
        def _():
            for i in range(SPLIT):
                own_dn(i, t - 1).wait_send()
            all_up(t - 1).wait_send()

        @pl.when(t >= 2)
        def _():
            xr(t - 1).wait_send()
            xl(t - 1).wait_send()

        @pl.when(t >= 3)
        def _():
            rel_r(t - 2).wait_send()
            rel_l(t - 2).wait_send()

        return 0

    def relay(t):
        xr(t).wait_recv()
        xl(t).wait_recv()
        rel_r(t).start()
        rel_l(t).start()

    lax.fori_loop(1, HALF + 1, tick, 0)

    fill(0, [gb[2, 13], gb[2, 14], gb[0, 13], gb[0, 14]])
    rel_r(HALF - 2).wait_recv()
    rel_l(HALF - 2).wait_recv()
    fill(96, [gb[1, 11], gb[1, 12]])
    nearest(0, 144)
    for copy in own_a + own_b:
        copy.wait_send()
    for copy in last_b:
        copy.wait_recv()
    rel_r(HALF - 1).wait_recv()
    rel_l(HALF - 1).wait_recv()
    fill(0, [gb[1, 13], gb[1, 14], gb[0, 15], gb[1, 15], gb[2, 15], gb[2, 15, 0:8]])
    nearest(0, 128)
    rel_r(HALF - 1).wait_send()
    rel_l(HALF - 1).wait_send()

    low = jnp.min(acc[...], axis=0, keepdims=True)
    low = (low + pn[...]) / width
    for i in range(npts // 128):
        mins[0, i : i + 1, :] = low[:, 128 * i : 128 * i + 128]
    swaps = [remote(mins.at[0], mins.at[j], scm.at[j], rcm.at[j], mate(j)) for j in range(1, NC)]
    for copy in swaps:
        copy.start()
    for copy in last_b:
        copy.wait_send()
    new = jnp.minimum(prior_ref[...], mins[0])
    for copy in swaps:
        copy.wait_recv()
    for j in range(1, NC):
        new = jnp.minimum(new, mins[j])
    out_ref[...] = new

    sx[x] = jnp.sum(new, axis=0, keepdims=True)
    sums = [
        remote(sx.at[x], sx.at[x], scx.at[d], rcx.at[d], peer(0, d)) for d in range(1, NX)
    ]
    for copy in sums:
        copy.start()
    for copy in swaps:
        copy.wait_send()
    for d in range(1, NX):
        src = lax.rem(x - d + NX, NX)
        remote(sx.at[x], sx.at[src], scx.at[d], rcx.at[d], peer(0, d)).wait_recv()
    sz[z] = (sx[0] + sx[1]) + (sx[2] + sx[3])
    sumz = [
        remote(sz.at[z], sz.at[z], scz.at[d], rcz.at[d], peer(d, 0)) for d in range(1, NZ)
    ]
    for copy in sumz:
        copy.start()
    for copy in sums:
        copy.wait_send()
    for d in range(1, NZ):
        src = lax.rem(z - d + NZ, NZ)
        remote(sz.at[z], sz.at[src], scz.at[d], rcz.at[d], peer(d, 0)).wait_recv()
    total = sz[0]
    for i in range(1, NZ):
        total = total + sz[i]
    cost_ref[...] = jnp.broadcast_to(
        jnp.sum(total, axis=1, keepdims=True) / (npts * NZ * NX), cost_ref.shape
    )
    for copy in sumz:
        copy.wait_send()


def hbm(array):
    return pltpu.with_memory_space_constraint(array, pltpu.HBM)


def local(points, prior_min, cand_slots):
    npts, width = points.shape
    vmem = pl.BlockSpec(memory_space=pltpu.VMEM)
    dma = pltpu.SemaphoreType.DMA
    new, cost = pl.pallas_call(
        kernel,
        out_shape=(
            jax.ShapeDtypeStruct((npts // 128, 128), F32),
            jax.ShapeDtypeStruct((1, 128), F32),
        ),
        in_specs=[pl.BlockSpec(memory_space=pltpu.HBM)] * 3,
        out_specs=(vmem, vmem),
        scratch_shapes=[
            pltpu.SMEM((RA + RB,), jnp.int32),
            pltpu.VMEM((npts // 128, 128), F32),
            pltpu.VMEM((npts, width), F32),
            pltpu.VMEM((3 * width, npts), BF16),
            pltpu.VMEM((1, npts), F32),
            pltpu.VMEM((NZ, RA + RB, width), F32),
            pltpu.VMEM((NZ + 1, NX - 1, RA, width), F32),
            pltpu.VMEM((NX - 1, NZ, RB, width), F32),
            pltpu.VMEM((256, 3 * width), BF16),
            pltpu.VMEM((256, 128), F32),
            pltpu.VMEM((8, npts), F32),
            pltpu.VMEM((NC, npts // 128, 128), F32),
            pltpu.VMEM((NX, 1, 128), F32),
            pltpu.VMEM((NZ, 1, 128), F32),
            dma((6,)), dma((10, 2)),
            dma((SPLIT, 2, HALF + 1)), dma((2, HALF + 1)), dma((2, HALF + 1)), dma((2, HALF + 1)),
            dma((3,)), dma((6,)), dma((9,)),
            dma((NC,)), dma((NC,)), dma((NX,)), dma((NX,)), dma((NZ,)), dma((NZ,)),
        ],
        compiler_params=pltpu.CompilerParams(
            collective_id=0, has_side_effects=True, vmem_limit_bytes=48 << 20
        ),
    )(hbm(points), hbm(prior_min.reshape(npts // 128, 128)), hbm(cand_slots.reshape(-1)))
    return new.reshape(-1), cost[0, 0]


def solution(mesh):
    placed = (P("pts", None), P("pts"), P("pts", "cand", None))
    return jax.shard_map(
        local, mesh=mesh, in_specs=placed, out_specs=(P("pts"), P()), check_vma=False
    )
```

time: 75.7 us -> 68.6 us (0.906)
  local copies, waits for them, and re-layouts: 4.13 us -> 0.6 us
  Pallas kernels: 69.5 us -> 66 us
    pallas_call x1, Pallas kernels: 69.5 us -> 66 us  [local(): pl.pallas_call(kernel, out_shape=(jax.ShapeDtypeStruct((npts // 128, 128)...]
    unnamed x7 -> x1, local copies, waits for them, and re-layouts: 4.13 us -> 0.6 us
where the time goes in v2:
time: 68.6 us; the launch traced here: 68.4 us
  Pallas kernels  66 us (96%)
  between operations  1.8 us (3%)
    pallas_call x1, Pallas kernels, local(): pl.pallas_call(kernel, out_shape=(jax.ShapeDtypeStruct((npts // 128, 128)...  66 us

profile of v2, /device:TPU:1, one launch (start us, length us, event | category | flops | bytes accessed | tf_op | source)
XLA Modules:
  0.0 68.4 jit_solution(17069350113063987619)
XLA Ops:
  0.6 66.0 %shard_map.50 = (f32[16,128]{1,0:T(8,128)S(1)}, f32[1,128]{1,0:T(1,128)S(1)}) custom-call(f32[2048,512]{1,0:T(8,128)} %pts_hbm.1, f32[16,128]{1,0:T(8,128)} %bitcast.7, s32[32]{0:T(128)} %bitcast.8), custom_call_target="tpu_custom_call" | custom-call | tf_op jit(solution)/shard_map/pallas_call | solution.py:341
  66.6 0.6 copy.7

commit v3 on v2

--- a/solution.py
+++ b/solution.py
@@ -15,10 +15,14 @@
 F32, BF16 = jnp.float32, jnp.bfloat16
 
 
+def when(condition):
+    return lambda body: body() if condition else None
+
+
 def kernel(
     pts_hbm, prior_hbm, slots_hbm, out_ref, cost_ref,
-    slots_ref, prior_ref, pf, p3, pn, own, ga, gb, c3, cnb, acc, mins, sx, sz,
-    load_sem, ssem, rown, rall, rx, rr, rax, rbx, s0, scm, rcm, scx, rcx, scz, rcz,
+    slots_ref, prior_ref, pf, p3, pn, own, ga, gb, c3, cnb, acc, mins, sz,
+    load_sem, ssem, rown, rall, rx, rr, rax, rbx, s0, scm, rcm, scz, rcz,
 ):
     p, c = lax.axis_index("pts"), lax.axis_index("cand")
     z, x = p // NX, p % NX
@@ -37,6 +41,7 @@
             device_id=where, device_id_type=MESH,
         )
 
+    zu, zd, xu, xd = peer(-1, 0), peer(1, 0), peer(0, 1), peer(0, -1)
     loads = []
     for q in range(4):
         rows = pl.ds(q * quarter, quarter)
@@ -67,43 +72,43 @@
     pl.semaphore_wait(barrier, len(near))
 
     def up(t):
-        return jnp.maximum(2 * t - 1, 0)
+        return max(2 * t - 1, 0)
 
     def sent(kind, t):
-        return ssem.at[kind, lax.rem(t, 2)]
+        return ssem.at[kind, t % 2]
 
     parts = [pl.ds(i * (RA + RB) // SPLIT, (RA + RB) // SPLIT) for i in range(SPLIT)]
 
     def own_up(i, t):
         src, dst = own.at[up(t), parts[i]], own.at[2 * t + 1, parts[i]]
-        return remote(src, dst, sent(i, t), rown.at[i, 0, t + 1], peer(-1, 0))
+        return remote(src, dst, sent(i, t), rown.at[i, 0, t + 1], zu)
 
     def own_dn(i, t):
         src, dst = own.at[2 * t, parts[i]], own.at[2 * t + 2, parts[i]]
-        return remote(src, dst, sent(2 + i, t), rown.at[i, 1, t + 1], peer(1, 0))
+        return remote(src, dst, sent(2 + i, t), rown.at[i, 1, t + 1], zd)
 
     def all_up(t):
-        return remote(ga.at[up(t)], ga.at[2 * t + 1], sent(4, t), rall.at[0, t + 1], peer(-1, 0))
+        return remote(ga.at[up(t)], ga.at[2 * t + 1], sent(4, t), rall.at[0, t + 1], zu)
 
     def all_dn(t):
-        return remote(ga.at[2 * t], ga.at[2 * t + 2], sent(5, t), rall.at[1, t + 1], peer(1, 0))
+        return remote(ga.at[2 * t], ga.at[2 * t + 2], sent(5, t), rall.at[1, t + 1], zd)
 
     def xr(t):
         two = pl.ds(2 * t - 1, 2)
         src = own.at[two, pl.ds(RA, RB)]
-        return remote(src, gb.at[2, two], sent(6, t), rx.at[0, t], peer(0, 1))
+        return remote(src, gb.at[2, two], sent(6, t), rx.at[0, t], xu)
 
     def xl(t):
         two = pl.ds(2 * t - 1, 2)
         src = own.at[two, pl.ds(RA, RB)]
-        return remote(src, gb.at[0, two], sent(7, t), rx.at[1, t], peer(0, -1))
+        return remote(src, gb.at[0, two], sent(7, t), rx.at[1, t], xd)
 
     def rel_r(t):
         at = 2 * t - 1
-        return remote(gb.at[2, at], gb.at[1, at], sent(8, t), rr.at[0, t], peer(0, 1))
+        return remote(gb.at[2, at], gb.at[1, at], sent(8, t), rr.at[0, t], xu)
 
     def rel_l(t):
-        return remote(gb.at[0, 2 * t], gb.at[1, 2 * t], sent(9, t), rr.at[1, t], peer(0, -1))
+        return remote(gb.at[0, 2 * t], gb.at[1, 2 * t], sent(9, t), rr.at[1, t], xd)
 
     around = (3, 1, 2)
     own_a = [
@@ -168,63 +173,63 @@
         for i in range(SPLIT):
             own_up(i, t - 1).wait_recv()
 
-            @pl.when(t < HALF)
+            @when(t < HALF)
             def _():
                 own_up(i, t).start()
                 own_dn(i, t - 1).wait_recv()
 
-            @pl.when(t < HALF - 1)
+            @when(t < HALF - 1)
             def _():
                 own_dn(i, t).start()
 
-        @pl.when(t < HALF)
+        @when(t < HALF)
         def _():
             xr(t).start()
             xl(t).start()
             fill(0, [own[2 * t - 1], own[2 * t]])
 
-        @pl.when(t == HALF)
+        @when(t == HALF)
         def _():
             for copy in last_b:
                 copy.start()
             fill(0, [own[far], own[far]])
 
-        @pl.when(t == 1)
+        @when(t == 1)
         def _():
             for copy in own_b:
                 copy.wait_recv()
             fill(64, [gb[0, 0], gb[1, 0], gb[2, 0], others(0)])
 
-        @pl.when(t >= 3)
+        @when(t >= 3)
         def _():
             fill(64, [gb[2, 2 * t - 5], gb[2, 2 * t - 4], gb[0, 2 * t - 5], gb[0, 2 * t - 4]])
 
         nearest(0, 160)
 
-        @pl.when(t == HALF)
+        @when(t == HALF)
         def _():
             relay(t - 1)
 
         all_dn(t - 1).wait_recv()
 
-        @pl.when(t < HALF)
+        @when(t < HALF)
         def _():
             all_dn(t).start()
             all_up(t - 1).wait_recv()
 
-        @pl.when(t < HALF - 1)
+        @when(t < HALF - 1)
         def _():
             all_up(t).start()
 
-        @pl.when(t < HALF)
+        @when(t < HALF)
         def _():
             fill(160, [others(2 * t - 1), others(2 * t)])
 
-        @pl.when(t == HALF)
+        @when(t == HALF)
         def _():
             fill(160, [others(2 * HALF), others(2 * HALF)])
 
-        @pl.when(t >= 4)
+        @when(t >= 4)
         def _():
             rel_r(t - 3).wait_recv()
             rel_l(t - 3).wait_recv()
@@ -232,7 +237,7 @@
 
         nearest(160, 96)
 
-        @pl.when((t >= 2) & (t < HALF))
+        @when(t >= 2 and t < HALF)
         def _():
             relay(t - 1)
 
@@ -240,18 +245,18 @@
             own_up(i, t - 1).wait_send()
         all_dn(t - 1).wait_send()
 
-        @pl.when(t < HALF)
+        @when(t < HALF)
         def _():
             for i in range(SPLIT):
                 own_dn(i, t - 1).wait_send()
             all_up(t - 1).wait_send()
 
-        @pl.when(t >= 2)
+        @when(t >= 2)
         def _():
             xr(t - 1).wait_send()
             xl(t - 1).wait_send()
 
-        @pl.when(t >= 3)
+        @when(t >= 3)
         def _():
             rel_r(t - 2).wait_send()
             rel_l(t - 2).wait_send()
@@ -264,7 +269,8 @@
         rel_r(t).start()
         rel_l(t).start()
 
-    lax.fori_loop(1, HALF + 1, tick, 0)
+    for t in range(1, HALF + 1):
+        tick(t, 0)
 
     fill(0, [gb[2, 13], gb[2, 14], gb[0, 13], gb[0, 14]])
     rel_r(HALF - 2).wait_recv()
@@ -298,35 +304,26 @@
         new = jnp.minimum(new, mins[j])
     out_ref[...] = new
 
-    sx[x] = jnp.sum(new, axis=0, keepdims=True)
-    sums = [
-        remote(sx.at[x], sx.at[x], scx.at[d], rcx.at[d], peer(0, d)) for d in range(1, NX)
-    ]
+    sz[p] = jnp.sum(new, axis=0, keepdims=True)
+    order = sorted(range(1, NZ * NX), key=lambda d: -(min(d // NX, NZ - d // NX) + min(d % NX, NX - d % NX)))
+
+    def total_at(i, slot):
+        d = order[i]
+        return remote(sz.at[p], sz.at[slot], scz.at[i], rcz.at[i], peer(d // NX, d % NX))
+
+    sums = [total_at(i, p) for i in range(NZ * NX - 1)]
     for copy in sums:
         copy.start()
     for copy in swaps:
         copy.wait_send()
-    for d in range(1, NX):
-        src = lax.rem(x - d + NX, NX)
-        remote(sx.at[x], sx.at[src], scx.at[d], rcx.at[d], peer(0, d)).wait_recv()
-    sz[z] = (sx[0] + sx[1]) + (sx[2] + sx[3])
-    sumz = [
-        remote(sz.at[z], sz.at[z], scz.at[d], rcz.at[d], peer(d, 0)) for d in range(1, NZ)
-    ]
-    for copy in sumz:
-        copy.start()
-    for copy in sums:
-        copy.wait_send()
-    for d in range(1, NZ):
-        src = lax.rem(z - d + NZ, NZ)
-        remote(sz.at[z], sz.at[src], scz.at[d], rcz.at[d], peer(d, 0)).wait_recv()
-    total = sz[0]
-    for i in range(1, NZ):
-        total = total + sz[i]
+    for i, d in enumerate(order):
+        src = lax.rem(z - d // NX + NZ, NZ) * NX + lax.rem(x - d % NX + NX, NX)
+        total_at(i, src).wait_recv()
+    total = jnp.sum(sz[...], axis=0)
     cost_ref[...] = jnp.broadcast_to(
         jnp.sum(total, axis=1, keepdims=True) / (npts * NZ * NX), cost_ref.shape
     )
-    for copy in sumz:
+    for copy in sums:
         copy.wait_send()
 
 
@@ -359,12 +356,11 @@
             pltpu.VMEM((256, 128), F32),
             pltpu.VMEM((8, npts), F32),
             pltpu.VMEM((NC, npts // 128, 128), F32),
-            pltpu.VMEM((NX, 1, 128), F32),
-            pltpu.VMEM((NZ, 1, 128), F32),
+            pltpu.VMEM((NZ * NX, 1, 128), F32),
             dma((6,)), dma((10, 2)),
             dma((SPLIT, 2, HALF + 1)), dma((2, HALF + 1)), dma((2, HALF + 1)), dma((2, HALF + 1)),
             dma((3,)), dma((6,)), dma((9,)),
-            dma((NC,)), dma((NC,)), dma((NX,)), dma((NX,)), dma((NZ,)), dma((NZ,)),
+            dma((NC,)), dma((NC,)), dma((NZ * NX,)), dma((NZ * NX,)),
         ],
         compiler_params=pltpu.CompilerParams(
             collective_id=0, has_side_effects=True, vmem_limit_bytes=48 << 20

time: 68.6 us -> 67.9 us (0.990)
  Pallas kernels: 66 us -> 65.3 us
where the time goes in v3:
time: 67.9 us; the launch traced here: 67.7 us
  Pallas kernels  65.3 us (96%)
  between operations  1.8 us (3%)
    pallas_call x1, Pallas kernels, local(): pl.pallas_call(kernel, out_shape=(jax.ShapeDtypeStruct((npts // 128, 128)...  65.3 us

profile of v3, /device:TPU:1, one launch (start us, length us, event | category | flops | bytes accessed | tf_op | source)
XLA Modules:
  0.0 67.7 jit_solution(54005975098032066)
XLA Ops:
  0.6 65.3 %shard_map.50 = (f32[16,128]{1,0:T(8,128)S(1)}, f32[1,128]{1,0:T(1,128)S(1)}) custom-call(f32[2048,512]{1,0:T(8,128)} %pts_hbm.1, f32[16,128]{1,0:T(8,128)} %bitcast.7, s32[32]{0:T(128)} %bitcast.8), custom_call_target="tpu_custom_call" | custom-call | tf_op jit(solution)/shard_map/pallas_call | solution.py:338
  65.9 0.6 copy.7

commit v4 on v3

--- a/solution.py
+++ b/solution.py
@@ -316,15 +316,15 @@
         copy.start()
     for copy in swaps:
         copy.wait_send()
-    for i, d in enumerate(order):
+    for copy in sums:
+        copy.wait_send()
+    for i, d in reversed(list(enumerate(order))):
         src = lax.rem(z - d // NX + NZ, NZ) * NX + lax.rem(x - d % NX + NX, NX)
         total_at(i, src).wait_recv()
     total = jnp.sum(sz[...], axis=0)
     cost_ref[...] = jnp.broadcast_to(
         jnp.sum(total, axis=1, keepdims=True) / (npts * NZ * NX), cost_ref.shape
     )
-    for copy in sums:
-        copy.wait_send()
 
 
 def hbm(array):

time: 67.9 us -> 67.7 us (level)
  no operation moved by 1% of the time
where the time goes in v4:
time: 67.7 us; the launch traced here: 67.5 us
  Pallas kernels  65.1 us (96%)
  between operations  1.8 us (3%)
    pallas_call x1, Pallas kernels, local(): pl.pallas_call(kernel, out_shape=(jax.ShapeDtypeStruct((npts // 128, 128)...  65.1 us

profile of v4, /device:TPU:1, one launch (start us, length us, event | category | flops | bytes accessed | tf_op | source)
XLA Modules:
  0.0 67.5 jit_solution(9668799331907775666)
XLA Ops:
  0.6 65.1 %shard_map.50 = (f32[16,128]{1,0:T(8,128)S(1)}, f32[1,128]{1,0:T(1,128)S(1)}) custom-call(f32[2048,512]{1,0:T(8,128)} %pts_hbm.1, f32[16,128]{1,0:T(8,128)} %bitcast.7, s32[32]{0:T(128)} %bitcast.8), custom_call_target="tpu_custom_call" | custom-call | tf_op jit(solution)/shard_map/pallas_call | solution.py:338
  65.7 0.6 copy.7

commit v5 on v4

--- a/solution.py
+++ b/solution.py
@@ -42,25 +42,23 @@
         )
 
     zu, zd, xu, xd = peer(-1, 0), peer(1, 0), peer(0, 1), peer(0, -1)
+    barrier = pltpu.get_barrier_semaphore()
+    near = [peer(1, 0), peer(-1, 0), peer(0, 1), peer(0, -1), peer(0, 2)]
+    near += [mate(j) for j in range(1, NC)]
+    for who in near:
+        pl.semaphore_signal(barrier, inc=1, device_id=who, device_id_type=MESH)
     loads = []
     for q in range(4):
         rows = pl.ds(q * quarter, quarter)
         load = pltpu.make_async_copy(pts_hbm.at[rows], pf.at[rows], load_sem.at[q])
         load.start()
         loads.append(load)
-
-    barrier = pltpu.get_barrier_semaphore()
-    near = [peer(1, 0), peer(-1, 0), peer(0, 1), peer(0, -1), peer(0, 2)]
-    near += [mate(j) for j in range(1, NC)]
-    for who in near:
-        pl.semaphore_signal(barrier, inc=1, device_id=who, device_id_type=MESH)
     slots_copy = pltpu.make_async_copy(slots_hbm, slots_ref, load_sem.at[4])
     slots_copy.start()
     prior_copy = pltpu.make_async_copy(prior_hbm, prior_ref, load_sem.at[5])
     prior_copy.start()
     acc[...] = jnp.full(acc.shape, 3e38, F32)
     slots_copy.wait()
-    prior_copy.wait()
     for load in loads:
         load.wait()
 
@@ -297,6 +295,7 @@
         copy.start()
     for copy in last_b:
         copy.wait_send()
+    prior_copy.wait()
     new = jnp.minimum(prior_ref[...], mins[0])
     for copy in swaps:
         copy.wait_recv()

time: 67.7 us -> 67.8 us (level)
  no operation moved by 1% of the time
where the time goes in v5:
time: 67.8 us; the launch traced here: 67.6 us
  Pallas kernels  65.2 us (96%)
  between operations  1.8 us (3%)
    pallas_call x1, Pallas kernels, local(): pl.pallas_call(kernel, out_shape=(jax.ShapeDtypeStruct((npts // 128, 128)...  65.2 us

profile of v5, /device:TPU:1, one launch (start us, length us, event | category | flops | bytes accessed | tf_op | source)
XLA Modules:
  0.0 67.6 jit_solution(7401385007975523187)
XLA Ops:
  0.6 65.2 %shard_map.50 = (f32[16,128]{1,0:T(8,128)S(1)}, f32[1,128]{1,0:T(1,128)S(1)}) custom-call(f32[2048,512]{1,0:T(8,128)} %pts_hbm.1, f32[16,128]{1,0:T(8,128)} %bitcast.7, s32[32]{0:T(128)} %bitcast.8), custom_call_target="tpu_custom_call" | custom-call | tf_op jit(solution)/shard_map/pallas_call | solution.py:337
  65.9 0.6 copy.7
